TPU v7x, 32 devices: a whole 2x2x4 slice. The times are simulated.
32 devices in a mesh: tm: 16 (over z, x, core), space: 2 (over y).
Axes of the slice: x: 2, y: 2, z: 4, core: 2. Of those that a mesh axis runs over, the one named last changes fastest.
Arguments:
- adjoint: float32 [16, 5, 4, 4, 4, 256], P('tm', None, None, None, None, 'space'), may hold values from -6 to 6
- gradient: float32 [16, 5, 4, 4, 4, 256], P('tm', None, None, None, None, 'space'), may hold values from -6 to 6
- jacobian: float32 [16, 3, 5, 5, 4, 4, 4, 256], P('tm', None, None, None, None, None, None, 'space'), may hold values from -0.3 to 0.3
- pseudo_step: float32 [16, 256], P('tm', 'space'), may hold values from 0.05 to 0.2
- send_list: int32 [512], P('space'), may hold values from 0 to 767, as said below
- face_source: int32 [6, 256], P(None, 'space'), may hold values from 0 to 1024, as said below
- coarse_owner: int32 [256, 1], P('space'), may hold values from 0 to 1; in each aligned block of 128 rows (0 to 127, 128 to 255, ...) at most 96 rows name the same one
- coarse_inv: float32 [16, 40, 40, 384], P('tm', None, None, 'space')
Outputs:
- adjoint_next: float32 [16, 5, 4, 4, 4, 256], P('tm', None, None, None, None, 'space')
Inputs may be any that keep to these rules, and one draw needn't show every extreme that they name: Each partition's face_source names slots of the previous and of the next partition's packed blocks for some of its faces; the rest of its faces take own columns or the zero column. `send_list`: entries are columns of the partition's own trace table. `coarse_owner`: at most 96 elements of one partition have the same owner; some owner receives exactly 96 from some partition.
All inputs are finite; a program needn't handle non-finite values.
Results may differ from a plain program's by a relative error of at most 0.0001.
Values sent between devices are 32-bit elements; how exact they have to be, the bound alone decides.
A program may use at most 64 MiB of HBM per device.

v0:
```python
import functools

import jax
import jax.numpy as jnp
import ml_dtypes
import numpy as np
from jax import lax
from jax.experimental import pallas as pl
from jax.experimental.pallas import tpu as pltpu
from jax.sharding import PartitionSpec as P

MESH = pl.DeviceIdType.MESH
f32, bf16 = jnp.float32, jnp.bfloat16
LANES = 128


def node_points(n):
    return np.linspace(-1.0, 1.0, n)


def lagrange(anchor, target):
    matrix = np.ones((len(target), len(anchor)))
    for c in range(len(anchor)):
        for k in range(len(anchor)):
            if k != c:
                matrix[:, c] = matrix[:, c] * (target - anchor[k]) / (anchor[c] - anchor[k])
    return matrix


def derivative(n):
    points = node_points(n)
    weights = np.ones(n)
    for j in range(n):
        for k in range(n):
            if k != j:
                weights[j] = weights[j] / (points[j] - points[k])
    matrix = np.zeros((n, n))
    for i in range(n):
        for j in range(n):
            if i != j:
                matrix[i, j] = weights[j] / weights[i] / (points[i] - points[j])
        matrix[i, i] = -np.sum(matrix[i])
    return matrix


def coupling_row(count):
    row = []
    for k in range(count):
        d = 0.0 if k == 0 else 0.5 * (-1) ** k * np.cos(np.pi * k / count) / np.sin(np.pi * k / count)
        row.append(float(0.25 * d + 2.0 * ((k == 0) - 1.0 / count)))
    return row


def kron3(a, b, c):
    return np.kron(np.kron(a, b), c)


def pad_to(matrix, rows, cols):
    out = np.zeros((rows, cols))
    out[: matrix.shape[0], : matrix.shape[1]] = matrix
    return out


def split_cat(matrix):
    hi = matrix.astype(np.float32).astype(ml_dtypes.bfloat16)
    lo = (matrix.astype(np.float32) - hi.astype(np.float32)).astype(ml_dtypes.bfloat16)
    return np.concatenate([hi, lo, hi], axis=1)


def face_select(n, rows):
    select = np.zeros((96, rows))
    for f in range(6):
        axis, end = f // 2, (f % 2) * (n - 1)
        count = 0
        for r in range(n):
            for s in range(n):
                index = [r, s]
                index.insert(axis, end)
                select[16 * f + count, (index[0] * n + index[1]) * n + index[2]] = 1.0
                count += 1
    return select


def deriv_cat(n, rows):
    dt, one = derivative(n).T, np.eye(n)
    return np.concatenate(
        [pad_to(m, rows, rows) for m in (kron3(dt, one, one), kron3(one, dt, one), kron3(one, one, dt))],
        axis=1,
    )


@functools.cache
def constants():
    p43 = lagrange(node_points(3), node_points(4))
    p32 = lagrange(node_points(2), node_points(3))
    q34 = lagrange(node_points(4), node_points(3))
    p43k, p32k, q34k = kron3(p43, p43, p43), kron3(p32, p32, p32), kron3(q34, q34, q34)
    e4, e3 = face_select(4, 64), face_select(3, 32)
    tables = {
        "e4": e4,
        "e3": e3,
        "d4": split_cat(deriv_cat(4, 64)),
        "d3": split_cat(deriv_cat(3, 32)),
        "et4": np.concatenate([e4.T, e4.T], axis=1),
        "et3": np.concatenate([e3.T, e3.T], axis=1),
        "r43": split_cat(pad_to(p43k.T, 32, 64)),
        "p43": split_cat(pad_to(p43k, 64, 32)),
        "r32": split_cat(pad_to(p32k.T, 16, 32)),
        "p32": split_cat(pad_to(p32k, 32, 8)),
        "q34": split_cat(pad_to(q34k, 32, 64)),
    }
    where, pieces, at = {}, [], 0
    for name, table in tables.items():
        where[name] = (at, table.shape[0], table.shape[1])
        pieces.append(pad_to(table.astype(np.float64), table.shape[0], 640))
        at += table.shape[0]
    return where, np.concatenate(pieces, axis=0).astype(ml_dtypes.bfloat16)


def dot(a, b):
    return jnp.dot(a, b, preferred_element_type=f32)


def split(x):
    hi = x.astype(bf16)
    return hi, (x - hi.astype(f32)).astype(bf16)


def split_rows(x):
    hi, lo = split(x)
    return jnp.concatenate([hi, hi, lo], axis=0)


def lane_cat(parts):
    return jnp.concatenate(parts, axis=1)


def kernel(nt, parts, cap, where, row, *refs):
    (adj, grad, jac, tau_ref, send_ref, face_ref, owner_ref, inv, const, out,
     jm, pick, jump_w, far_w, pack_w, rows_f, rows_m, sol, *rest) = refs
    fine_t = [rest[4 * i:4 * i + 4] for i in range(2)]
    mid_t = [rest[8 + 4 * i:12 + 4 * i] for i in range(5)]
    trace_out, trace_in, low_out, low_in, low_back = rest[28:33]
    t_send, t_recv, b_send, b_recv, h_send, h_recv, c_send, c_recv, g_send, g_recv = rest[33:]
    me_t, me_s = lax.axis_index("tm"), lax.axis_index("space")
    columns = LANES
    width = 5 * columns
    slots = send_ref.shape[1] // 2
    faces = 6 * columns
    cols = inv.shape[2]

    def mat(name):
        at, height, wide = where[name]
        return const[at:at + height, 0:wide]

    barrier = pltpu.get_barrier_semaphore()
    for k in range(1, nt):
        pl.semaphore_signal(barrier, inc=1, device_id={"tm": lax.rem(me_t + k, nt)}, device_id_type=MESH)
    for k in range(1, parts):
        pl.semaphore_signal(barrier, inc=1, device_id={"space": lax.rem(me_s + k, parts)}, device_id_type=MESH)
    pl.semaphore_wait(barrier, nt - 1 + parts - 1)

    def t_start(number, bufs, v):
        stage, landed, mixed, back = bufs
        piece = stage.shape[1]
        for k in range(nt):
            stage[k] = v[piece * k:piece * (k + 1), :]
        for k in range(1, nt):
            to = lax.rem(me_t + k, nt)
            pltpu.make_async_remote_copy(
                src_ref=stage.at[to], dst_ref=landed.at[nt - k], send_sem=t_send.at[number],
                recv_sem=t_recv.at[number], device_id={"tm": to}, device_id_type=MESH).start()
        landed[0] = stage[me_t]

    def all_of(buf, sem):
        view = buf.at[pl.ds(1, nt - 1)]
        pltpu.make_async_copy(view, view, sem).wait()

    def t_mix(number, bufs):
        stage, landed, mixed, back = bufs
        all_of(landed, t_recv.at[number])

        def block(b, carry):
            lanes = pl.ds(pl.multiple_of(b * LANES, LANES), LANES)
            y = landed[:, :, lanes]
            total = row[0] * y
            for m in range(1, nt):
                total = total + row[m] * jnp.concatenate([y[m:], y[:m]], axis=0)
            mixed[:, :, lanes] = total
            return carry

        lax.fori_loop(0, width // LANES, block, 0)
        for k in range(1, nt):
            to = lax.rem(me_t + k, nt)
            pltpu.make_async_remote_copy(
                src_ref=mixed.at[k], dst_ref=back.at[me_t], send_sem=b_send.at[number],
                recv_sem=b_recv.at[number], device_id={"tm": to}, device_id_type=MESH).start()
        back[me_t] = mixed[0]

    def t_finish(number, bufs, rows_ref):
        stage, landed, mixed, back = bufs
        all_of(back, b_recv.at[number])
        piece = stage.shape[1]
        for k in range(nt):
            rows_ref[piece * k:piece * (k + 1), :] = back[k]
        return rows_ref[...]

    def trace_copy(number, side):
        to = lax.rem(me_s + (parts - 1 if side == 0 else 1), parts)
        return pltpu.make_async_remote_copy(
            src_ref=trace_out.at[number, side], dst_ref=trace_in.at[number, 1 - side],
            send_sem=h_send.at[number, side], recv_sem=h_recv.at[number, 1 - side],
            device_id={"space": to}, device_id_type=MESH)

    def s_start(number, v, e_name):
        hi, lo = split(v)
        chosen = mat(e_name)
        t_hi, t_lo = dot(chosen, hi).astype(bf16), dot(chosen, lo).astype(bf16)
        table = jnp.concatenate(
            [lane_cat([t[16 * f:16 * f + 16, columns * i:columns * (i + 1)] for f in range(6)])
             for t in (t_hi, t_lo) for i in range(5)], axis=0)
        packed = dot(table, pick[...])
        packed = packed[:80] + packed[80:]
        for side in range(2):
            trace_out[number, side] = packed[:, slots * side:slots * (side + 1)]
            trace_copy(number, side).start()
        return table

    def flux(v, jac_at, d_name):
        w = []
        for a in range(3):
            total = jac_at[5 * a] * v[:, 0:columns][None]
            for i in range(1, 5):
                total = total + jac_at[5 * a + i] * v[:, columns * i:columns * (i + 1)][None]
            w.append(lane_cat([total[j] for j in range(5)]))
        return dot(mat(d_name), split_rows(jnp.concatenate(w, axis=0)))

    def s_local(table):
        jump = dot(table, jump_w[...])
        return jump[:80] + jump[80:]

    def s_finish(number, jump, et_name):
        for side in range(2):
            trace_copy(number, side).wait_recv()
        hi, lo = split(lane_cat([trace_in[number, 0], trace_in[number, 1]]))
        far = dot(jnp.concatenate([hi, lo], axis=0), far_w[...])
        jump = jump + far[:80] + far[80:]
        put = jnp.concatenate(
            [lane_cat([jump[16 * i:16 * i + 16, columns * f:columns * (f + 1)] for i in range(5)])
             for f in range(6)], axis=0)
        hi, lo = split(put)
        return dot(mat(et_name), jnp.concatenate([hi, lo], axis=0))

    v = lane_cat([adj[i] for i in range(5)])
    t_start(0, fine_t[0], v)
    rows768 = lax.broadcasted_iota(jnp.int32, (faces, 2 * slots), 0)
    pick[...] = jnp.where(rows768 == send_ref[...], 1.0, 0.0).astype(bf16)
    table = s_start(0, v, "e4")
    row_id = lax.broadcasted_iota(jnp.int32, (faces, columns), 0)
    lane_id = lax.broadcasted_iota(jnp.int32, (faces, columns), 1)
    far_id = lax.broadcasted_iota(jnp.int32, (2 * slots, columns), 0) + faces
    for f in range(6):
        source = face_ref[f:f + 1, :]
        own = jnp.where(row_id == lane_id + f * columns, 1.0, 0.0)
        jump_w[:, columns * f:columns * (f + 1)] = (own - jnp.where(row_id == source, 1.0, 0.0)).astype(bf16)
        far_w[:, columns * f:columns * (f + 1)] = jnp.where(far_id == source, -1.0, 0.0).astype(bf16)
    tau = lane_cat([tau_ref[...]] * 5)
    g = lane_cat([grad[i] for i in range(5)])
    part = flux(v, jac, "d4")
    jump = s_local(table)
    t_mix(0, fine_t[0])
    part = g - part - s_finish(0, jump, "et4")

    def to_mid(c, carry):
        picked = lane_cat([jac[c, j] for j in range(5)])
        small = dot(mat("q34"), split_rows(picked))
        for j in range(5):
            jm[c, j] = small[:, columns * j:columns * (j + 1)]
        return carry

    lax.fori_loop(0, 15, to_mid, 0)
    owners = owner_ref[...]
    lane_c = lax.broadcasted_iota(jnp.int32, (columns, LANES), 1)
    sub_c = lax.broadcasted_iota(jnp.int32, (columns, LANES), 0)
    named = jnp.where(owners == lane_c, 1.0, 0.0)
    before = dot(jnp.where(sub_c > lane_c, 1.0, 0.0).astype(bf16), named.astype(bf16))
    rank = jnp.sum(before * named, axis=1, keepdims=True)
    wide = pack_w.shape[2]
    lane_w = lax.broadcasted_iota(jnp.int32, (columns, wide), 1).astype(f32)
    slot = rank + (me_s * cap).astype(f32)
    for q in range(parts):
        pack_w[q] = jnp.where(jnp.logical_and(lane_w == slot, owners == q), 1.0, 0.0).astype(bf16)

    smoothed = v + tau * (part - t_finish(0, fine_t[0], rows_f))

    t_start(1, mid_t[0], dot(mat("r43"), split_rows(smoothed)))
    table = s_start(1, smoothed, "e4")
    t_start(2, fine_t[1], smoothed)
    part = flux(smoothed, jac, "d4")
    jump = s_local(table)
    t_mix(1, mid_t[0])
    part = g - part - s_finish(1, jump, "et4")
    rhs = dot(mat("r43"), split_rows(part)) - t_finish(1, mid_t[0], rows_m)

    def mid_residual(number, t_number, bufs, c, background=None):
        t_start(t_number, bufs, c)
        made = s_start(number, c, "e3")
        inner = flux(c, jm, "d3")
        step_jump = s_local(made)
        t_mix(t_number, bufs)
        if background is not None:
            background()
        inner = rhs - inner - s_finish(number, step_jump, "et3")
        return inner - t_finish(t_number, bufs, rows_m)

    c = tau * rhs
    c = c + tau * mid_residual(2, 3, mid_t[1], c, lambda: t_mix(2, fine_t[1]))
    left = mid_residual(3, 4, mid_t[2], c)

    low = dot(mat("r32"), split_rows(left))[:8]
    low = jnp.concatenate([low[:, columns * i:columns * (i + 1)] for i in range(5)], axis=0)
    hi, lo = split(low)
    stacked = jnp.concatenate([hi, lo], axis=0)

    def packed_for(q):
        both = dot(stacked, pack_w[q])
        return both[:40] + both[40:]

    def low_copy(k):
        return pltpu.make_async_remote_copy(
            src_ref=low_out.at[k], dst_ref=low_in.at[parts - k], send_sem=c_send.at[k],
            recv_sem=c_recv.at[parts - k], device_id={"space": lax.rem(me_s + k, parts)}, device_id_type=MESH)

    def back_copy(k):
        return pltpu.make_async_remote_copy(
            src_ref=sol, dst_ref=low_back.at[parts - k], send_sem=g_send.at[k],
            recv_sem=g_recv.at[parts - k], device_id={"space": lax.rem(me_s + k, parts)}, device_id_type=MESH)

    for k in range(1, parts):
        low_out[k] = packed_for(lax.rem(me_s + k, parts))
        low_copy(k).start()
    arrived = packed_for(me_s)
    for k in range(1, parts):
        low_copy(k).wait_recv()
    for k in range(1, parts):
        arrived = arrived + low_in[k]
    arrived = arrived[:, :cols]
    if wide > cols:
        sol[:, cols:] = jnp.zeros((40, wide - cols), f32)
    for i in range(40):
        sol[i:i + 1, :cols] = jnp.sum(inv[i] * arrived, axis=0, keepdims=True)
    for k in range(1, parts):
        back_copy(k).start()

    def unpacked(values, q):
        v_hi, v_lo = split(values)
        both = lax.dot_general(
            jnp.concatenate([v_hi, v_lo], axis=0), pack_w[q], (((1,), (1,)), ((), ())),
            preferred_element_type=f32)
        return both[:40] + both[40:]

    fix = unpacked(sol[...], me_s)
    for k in range(1, parts):
        back_copy(k).wait_recv()
    for k in range(1, parts):
        fix = fix + unpacked(low_back[k], lax.rem(me_s + k, parts))
    fix = lane_cat([fix[8 * i:8 * i + 8] for i in range(5)])
    hi = fix.astype(bf16).astype(f32)
    fix = jnp.concatenate([hi, hi, fix - hi], axis=0).astype(bf16)
    c = c + dot(mat("p32"), fix)

    c = c + tau * mid_residual(4, 5, mid_t[3], c)
    t_start(6, mid_t[4], c)
    corrected = smoothed + dot(mat("p43"), split_rows(c))
    table = s_start(5, corrected, "e4")
    part = flux(corrected, jac, "d4")
    jump = s_local(table)
    t_mix(6, mid_t[4])
    part = g - part - s_finish(5, jump, "et4")
    part = part - t_finish(2, fine_t[1], rows_f)
    coupled = dot(mat("p43"), split_rows(t_finish(6, mid_t[4], rows_m)))
    result = corrected + tau * (part - coupled)
    for i in range(5):
        out[i] = result[:, columns * i:columns * (i + 1)]

    order = [fine_t[0], mid_t[0], fine_t[1], mid_t[1], mid_t[2], mid_t[3], mid_t[4]]
    for number, bufs in enumerate(order):
        all_of(bufs[0], t_send.at[number])
        all_of(bufs[2], b_send.at[number])
    for number in range(6):
        for side in range(2):
            trace_copy(number, side).wait_send()
    for k in range(1, parts):
        low_copy(k).wait_send()
        back_copy(k).wait_send()


def on_device(nt, parts, where, table, row, adjoint, gradient, jacobian, pseudo_step, send_list,
              face_source, coarse_owner, coarse_inv):
    columns = adjoint.shape[-1]
    cols = coarse_inv.shape[-1]
    slots = send_list.shape[0] // 2
    wide = -(-cols // LANES) * LANES
    width = 5 * columns
    faces = 6 * columns
    vmem = pl.BlockSpec(memory_space=pltpu.VMEM)

    def time_buffers(rows):
        return [pltpu.VMEM((nt, rows // nt, width), f32) for _ in range(4)]

    scratch = [
        pltpu.VMEM((15, 5, 32, columns), f32),
        pltpu.VMEM((faces, 2 * slots), bf16),
        pltpu.VMEM((faces, faces), bf16),
        pltpu.VMEM((2 * slots, faces), bf16),
        pltpu.VMEM((parts, columns, wide), bf16),
        pltpu.VMEM((64, width), f32),
        pltpu.VMEM((32, width), f32),
        pltpu.VMEM((40, wide), f32),
    ]
    for rows in (64, 64, 32, 32, 32, 32, 32):
        scratch += time_buffers(rows)
    scratch += [
        pltpu.VMEM((6, 2, 80, slots), f32),
        pltpu.VMEM((6, 2, 80, slots), f32),
        pltpu.VMEM((parts, 40, wide), f32),
        pltpu.VMEM((parts, 40, wide), f32),
        pltpu.VMEM((parts, 40, wide), f32),
    ]
    dma = pltpu.SemaphoreType.DMA
    scratch += [dma((7,)) for _ in range(4)] + [dma((6, 2)) for _ in range(2)]
    scratch += [dma((parts,)) for _ in range(4)]
    result = pl.pallas_call(
        functools.partial(kernel, nt, parts, cols // parts, where, row),
        out_shape=jax.ShapeDtypeStruct((5, 64, columns), f32),
        in_specs=[vmem] * 9,
        out_specs=vmem,
        scratch_shapes=scratch,
        compiler_params=pltpu.CompilerParams(
            collective_id=0, has_side_effects=True, vmem_limit_bytes=50 * 1024 * 1024),
    )(
        adjoint.reshape(5, 64, columns),
        gradient.reshape(5, 64, columns),
        jacobian.reshape(15, 5, 64, columns),
        pseudo_step,
        send_list.reshape(1, 2 * slots),
        face_source,
        coarse_owner,
        coarse_inv.reshape(40, 40, cols),
        jnp.asarray(table),
    )
    return result.reshape(adjoint.shape)


def solution(mesh):
    nt, parts = mesh.shape["tm"], mesh.shape["space"]
    where, table = constants()
    placed = (
        P("tm", None, None, None, None, "space"),
        P("tm", None, None, None, None, "space"),
        P("tm", None, None, None, None, None, None, "space"),
        P("tm", "space"),
        P("space"),
        P(None, "space"),
        P("space", None),
        P("tm", None, None, "space"),
    )
    return jax.shard_map(
        functools.partial(on_device, nt, parts, where, table, coupling_row(nt)),
        mesh=mesh,
        in_specs=placed,
        out_specs=P("tm", None, None, None, None, "space"),
        check_vma=False,
    )
```

profile of v0, /device:TPU:0, one launch (start us, length us, event | category | flops | bytes accessed | tf_op | source)
XLA Modules:
  0.0 81.8 jit_solution(10993004654822076935)
XLA Ops:
  0.0 0.8 copy.10.refs_6_
  0.8 0.0 copy-start
  0.8 1.4 %copy-done = f32[1,40,40,192]{3,2,1,0:T(8,128)S(1)} copy-done((f32[1,40,40,192]{3,2,1,0:T(8,128)S(1)}, f32[1,40,40,192]{3,2,1,0:T(8,128)}, u32[]{:S(2)}) %copy-start) | copy-done | bytes 1228824
  2.2 0.0 copy-start.1
  2.2 1.1 %copy-done.1 = bf16[560,640]{1,0:T(8,128)(2,1)S(1)} copy-done((bf16[560,640]{1,0:T(8,128)(2,1)S(1)}, bf16[560,640]{1,0:T(8,128)(2,1)}, u32[]{:S(2)}) %copy-start.1) | copy-done | bytes 716824
  3.3 0.0 copy-start.2
  3.3 0.9 %copy-done.2 = f32[1,5,4,4,4,128]{5,4,3,2,1,0:T(4,128)S(1)} copy-done((f32[1,5,4,4,4,128]{5,4,3,2,1,0:T(4,128)S(1)}, f32[1,5,4,4,4,128]{5,4,3,2,1,0:T(4,128)}, u32[]{:S(2)}) %copy-start.2) | copy-done | bytes 163864
  4.2 0.0 copy-start.3
  4.2 0.9 %copy-done.3 = f32[1,5,4,4,4,128]{5,4,3,2,1,0:T(4,128)S(1)} copy-done((f32[1,5,4,4,4,128]{5,4,3,2,1,0:T(4,128)S(1)}, f32[1,5,4,4,4,128]{5,4,3,2,1,0:T(4,128)}, u32[]{:S(2)}) %copy-start.3) | copy-done | bytes 163864
  5.1 0.0 copy-start.4
  5.1 0.7 copy-done.4
  5.8 0.0 copy-start.5
  5.8 0.7 copy-done.5
  6.5 0.0 copy-start.6
  6.5 0.7 copy-done.6
  7.2 73.9 %shard_map.91 = f32[5,64,128]{2,1,0:T(8,128)S(1)} custom-call(f32[5,64,128]{2,1,0:T(8,128)S(1)} %bitcast.8, f32[5,64,128]{2,1,0:T(8,128)S(1)} %bitcast.9, f32[15,5,64,128]{3,2,1,0:T(8,128)} %bitcast.11, f32[1,128]{1,0:T(1,128)S(1)} %copy-done.6, s32[1,256]{1,0:T(1,128)S(1)} %bitcast.10, s32[6,128]{1,0:T(8,128)S(1)} %copy-done.4, s32[128,1]{1,0:T(8,128)S(1)} %copy.10.refs_6_, ...), custom_call_target="tpu_custom_call" | custom-call | tf_op jit(solution)/shard_map/pallas_call | solution.py:433
  81.1 0.7 copy.12
Async XLA Ops:
  0.8 1.4 %copy-start = (f32[1,40,40,192]{3,2,1,0:T(8,128)S(1)}, f32[1,40,40,192]{3,2,1,0:T(8,128)}, u32[]{:S(2)}) copy-start(f32[1,40,40,192]{3,2,1,0:T(8,128)} %param.16) | copy-start | bytes 3686404
  2.2 1.1 %copy-start.1 = (bf16[560,640]{1,0:T(8,128)(2,1)S(1)}, bf16[560,640]{1,0:T(8,128)(2,1)}, u32[]{:S(2)}) copy-start(bf16[560,640]{1,0:T(8,128)(2,1)} %constant.2.clone.refs_8_) | copy-start | bytes 2150404
  3.3 0.9 %copy-start.2 = (f32[1,5,4,4,4,128]{5,4,3,2,1,0:T(4,128)S(1)}, f32[1,5,4,4,4,128]{5,4,3,2,1,0:T(4,128)}, u32[]{:S(2)}) copy-start(f32[1,5,4,4,4,128]{5,4,3,2,1,0:T(4,128)} %param.9) | copy-start | bytes 491524
  4.2 0.9 %copy-start.3 = (f32[1,5,4,4,4,128]{5,4,3,2,1,0:T(4,128)S(1)}, f32[1,5,4,4,4,128]{5,4,3,2,1,0:T(4,128)}, u32[]{:S(2)}) copy-start(f32[1,5,4,4,4,128]{5,4,3,2,1,0:T(4,128)} %param.10) | copy-start | bytes 491524
  5.1 0.7 copy-start.4
  5.8 0.7 copy-start.5
  6.5 0.7 copy-start.6
where the time goes:
time: 82.1 us; the launch traced here: 81.8 us
  Pallas kernels  73.9 us (90%)
  local copies, waits for them, and re-layouts  7.81 us (10%)
    pallas_call x1, Pallas kernels, on_device(): pl.pallas_call(functools.partial(kernel, nt, parts, cols // parts, where,...  73.9 us
    unnamed x16, local copies, waits for them, and re-layouts  7.81 us

commit v1 on v0

--- a/solution.py
+++ b/solution.py
@@ -136,12 +136,13 @@
 
 
 def kernel(nt, parts, cap, where, row, *refs):
-    (adj, grad, jac, tau_ref, send_ref, face_ref, owner_ref, inv, const, out,
-     jm, pick, jump_w, far_w, pack_w, rows_f, rows_m, sol, *rest) = refs
-    fine_t = [rest[4 * i:4 * i + 4] for i in range(2)]
-    mid_t = [rest[8 + 4 * i:12 + 4 * i] for i in range(5)]
-    trace_out, trace_in, low_out, low_in, low_back = rest[28:33]
-    t_send, t_recv, b_send, b_recv, h_send, h_recv, c_send, c_recv, g_send, g_recv = rest[33:]
+    sources, out, held = refs[:9], refs[9], refs[10:19]
+    adj, grad, jac, tau_ref, send_ref, face_ref, owner_ref, inv, const = held
+    in_sem = refs[19]
+    (jm, pick, jump_w, far_w, pack_w, rows_f, rows_m, rows_l, sol, *rest) = refs[20:]
+    bufs_t = [rest[4 * i:4 * i + 4] for i in range(8)]
+    trace_out, trace_in, low_out, low_in, low_back = rest[32:37]
+    t_send, t_recv, b_send, b_recv, h_send, h_recv, c_send, c_recv, g_send, g_recv = rest[37:]
     me_t, me_s = lax.axis_index("tm"), lax.axis_index("space")
     columns = LANES
     width = 5 * columns
@@ -149,23 +150,31 @@
     faces = 6 * columns
     cols = inv.shape[2]
 
+    far_first = sorted(range(1, nt), key=lambda k: (-min(k, nt - k), k))
+
     def mat(name):
         at, height, wide = where[name]
         return const[at:at + height, 0:wide]
 
+    def fetch(i):
+        return pltpu.make_async_copy(sources[i], held[i], in_sem.at[i])
+
+    for i in (0, 4, 8, 5, 2, 1, 3, 6, 7):
+        fetch(i).start()
     barrier = pltpu.get_barrier_semaphore()
     for k in range(1, nt):
         pl.semaphore_signal(barrier, inc=1, device_id={"tm": lax.rem(me_t + k, nt)}, device_id_type=MESH)
     for k in range(1, parts):
         pl.semaphore_signal(barrier, inc=1, device_id={"space": lax.rem(me_s + k, parts)}, device_id_type=MESH)
+    fetch(0).wait()
     pl.semaphore_wait(barrier, nt - 1 + parts - 1)
 
-    def t_start(number, bufs, v):
-        stage, landed, mixed, back = bufs
+    def t_start(number, v):
+        stage, landed, mixed, back = bufs_t[number]
         piece = stage.shape[1]
         for k in range(nt):
             stage[k] = v[piece * k:piece * (k + 1), :]
-        for k in range(1, nt):
+        for k in far_first:
             to = lax.rem(me_t + k, nt)
             pltpu.make_async_remote_copy(
                 src_ref=stage.at[to], dst_ref=landed.at[nt - k], send_sem=t_send.at[number],
@@ -176,8 +185,8 @@
         view = buf.at[pl.ds(1, nt - 1)]
         pltpu.make_async_copy(view, view, sem).wait()
 
-    def t_mix(number, bufs):
-        stage, landed, mixed, back = bufs
+    def t_mix(number):
+        stage, landed, mixed, back = bufs_t[number]
         all_of(landed, t_recv.at[number])
 
         def block(b, carry):
@@ -189,16 +198,16 @@
             mixed[:, :, lanes] = total
             return carry
 
-        lax.fori_loop(0, width // LANES, block, 0)
-        for k in range(1, nt):
+        lax.fori_loop(0, landed.shape[2] // LANES, block, 0)
+        for k in far_first:
             to = lax.rem(me_t + k, nt)
             pltpu.make_async_remote_copy(
                 src_ref=mixed.at[k], dst_ref=back.at[me_t], send_sem=b_send.at[number],
                 recv_sem=b_recv.at[number], device_id={"tm": to}, device_id_type=MESH).start()
         back[me_t] = mixed[0]
 
-    def t_finish(number, bufs, rows_ref):
-        stage, landed, mixed, back = bufs
+    def t_finish(number, rows_ref):
+        stage, landed, mixed, back = bufs_t[number]
         all_of(back, b_recv.at[number])
         piece = stage.shape[1]
         for k in range(nt):
@@ -252,10 +261,13 @@
         return dot(mat(et_name), jnp.concatenate([hi, lo], axis=0))
 
     v = lane_cat([adj[i] for i in range(5)])
-    t_start(0, fine_t[0], v)
+    t_start(0, v)
+    fetch(4).wait()
     rows768 = lax.broadcasted_iota(jnp.int32, (faces, 2 * slots), 0)
     pick[...] = jnp.where(rows768 == send_ref[...], 1.0, 0.0).astype(bf16)
+    fetch(8).wait()
     table = s_start(0, v, "e4")
+    fetch(5).wait()
     row_id = lax.broadcasted_iota(jnp.int32, (faces, columns), 0)
     lane_id = lax.broadcasted_iota(jnp.int32, (faces, columns), 1)
     far_id = lax.broadcasted_iota(jnp.int32, (2 * slots, columns), 0) + faces
@@ -264,11 +276,13 @@
         own = jnp.where(row_id == lane_id + f * columns, 1.0, 0.0)
         jump_w[:, columns * f:columns * (f + 1)] = (own - jnp.where(row_id == source, 1.0, 0.0)).astype(bf16)
         far_w[:, columns * f:columns * (f + 1)] = jnp.where(far_id == source, -1.0, 0.0).astype(bf16)
+    for i in (2, 1, 3, 6):
+        fetch(i).wait()
     tau = lane_cat([tau_ref[...]] * 5)
     g = lane_cat([grad[i] for i in range(5)])
     part = flux(v, jac, "d4")
+    t_mix(0)
     jump = s_local(table)
-    t_mix(0, fine_t[0])
     part = g - part - s_finish(0, jump, "et4")
 
     def to_mid(c, carry):
@@ -280,50 +294,68 @@
 
     lax.fori_loop(0, 15, to_mid, 0)
     owners = owner_ref[...]
+    heads = max(8, parts)
+    owner_id = lax.broadcasted_iota(jnp.int32, (heads, columns), 0)
+    named = jnp.where(owner_id == owners, 1.0, 0.0)
     lane_c = lax.broadcasted_iota(jnp.int32, (columns, LANES), 1)
     sub_c = lax.broadcasted_iota(jnp.int32, (columns, LANES), 0)
-    named = jnp.where(owners == lane_c, 1.0, 0.0)
-    before = dot(jnp.where(sub_c > lane_c, 1.0, 0.0).astype(bf16), named.astype(bf16))
-    rank = jnp.sum(before * named, axis=1, keepdims=True)
-    wide = pack_w.shape[2]
-    lane_w = lax.broadcasted_iota(jnp.int32, (columns, wide), 1).astype(f32)
+    earlier = jnp.where(sub_c < lane_c, 1.0, 0.0).astype(bf16)
+    rank = jnp.sum(dot(named.astype(bf16), earlier) * named, axis=0, keepdims=True)
+    wide = pack_w.shape[1]
+    slot_id = lax.broadcasted_iota(jnp.int32, (wide, columns), 0).astype(f32)
     slot = rank + (me_s * cap).astype(f32)
     for q in range(parts):
-        pack_w[q] = jnp.where(jnp.logical_and(lane_w == slot, owners == q), 1.0, 0.0).astype(bf16)
-
-    smoothed = v + tau * (part - t_finish(0, fine_t[0], rows_f))
-
-    t_start(1, mid_t[0], dot(mat("r43"), split_rows(smoothed)))
+        pack_w[q] = jnp.where(jnp.logical_and(slot_id == slot, owners == q), 1.0, 0.0).astype(bf16)
+
+    smoothed = v + tau * (part - t_finish(0, rows_f))
+
+    t_start(1, dot(mat("r43"), split_rows(smoothed)))
     table = s_start(1, smoothed, "e4")
-    t_start(2, fine_t[1], smoothed)
     part = flux(smoothed, jac, "d4")
+    t_mix(1)
     jump = s_local(table)
-    t_mix(1, mid_t[0])
     part = g - part - s_finish(1, jump, "et4")
-    rhs = dot(mat("r43"), split_rows(part)) - t_finish(1, mid_t[0], rows_m)
-
-    def mid_residual(number, t_number, bufs, c, background=None):
-        t_start(t_number, bufs, c)
-        made = s_start(number, c, "e3")
-        inner = flux(c, jm, "d3")
-        step_jump = s_local(made)
-        t_mix(t_number, bufs)
-        if background is not None:
-            background()
-        inner = rhs - inner - s_finish(number, step_jump, "et3")
-        return inner - t_finish(t_number, bufs, rows_m)
+    rhs = dot(mat("r43"), split_rows(part)) - t_finish(1, rows_m)
+
+    def to_low(x):
+        x = dot(mat("r32"), split_rows(x))[:8]
+        return jnp.concatenate([x[:, columns * i:columns * (i + 1)] for i in range(5)], axis=0)
+
+    def from_low(x):
+        x = lane_cat([x[8 * i:8 * i + 8] for i in range(5)])
+        head = x.astype(bf16).astype(f32)
+        return dot(mat("p32"), jnp.concatenate([head, head, x - head], axis=0).astype(bf16))
+
+    def low_start(number, x):
+        extra = rows_l.shape[0] - 40
+        if extra:
+            x = jnp.concatenate([x, jnp.zeros((extra, columns), f32)], axis=0)
+        t_start(number, x)
 
     c = tau * rhs
-    c = c + tau * mid_residual(2, 3, mid_t[1], c, lambda: t_mix(2, fine_t[1]))
-    left = mid_residual(3, 4, mid_t[2], c)
-
-    low = dot(mat("r32"), split_rows(left))[:8]
-    low = jnp.concatenate([low[:, columns * i:columns * (i + 1)] for i in range(5)], axis=0)
+    t_start(3, c)
+    table = s_start(2, c, "e3")
+    part = flux(c, jm, "d3")
+    t_mix(3)
+    jump = s_local(table)
+    part = rhs - part - s_finish(2, jump, "et3")
+    c = c + tau * (part - t_finish(3, rows_m))
+
+    low_start(5, to_low(c))
+    table = s_start(3, c, "e3")
+    t_start(4, c)
+    part = flux(c, jm, "d3")
+    t_mix(5)
+    jump = s_local(table)
+    part = rhs - part - s_finish(3, jump, "et3")
+
+    low = to_low(part) - t_finish(5, rows_l)[:40]
     hi, lo = split(low)
     stacked = jnp.concatenate([hi, lo], axis=0)
 
     def packed_for(q):
-        both = dot(stacked, pack_w[q])
+        both = lax.dot_general(
+            stacked, pack_w[q], (((1,), (1,)), ((), ())), preferred_element_type=f32)
         return both[:40] + both[40:]
 
     def low_copy(k):
@@ -339,11 +371,14 @@
     for k in range(1, parts):
         low_out[k] = packed_for(lax.rem(me_s + k, parts))
         low_copy(k).start()
+    t_start(2, smoothed)
+    t_mix(4)
     arrived = packed_for(me_s)
     for k in range(1, parts):
         low_copy(k).wait_recv()
     for k in range(1, parts):
         arrived = arrived + low_in[k]
+    fetch(7).wait()
     arrived = arrived[:, :cols]
     if wide > cols:
         sol[:, cols:] = jnp.zeros((40, wide - cols), f32)
@@ -354,37 +389,39 @@
 
     def unpacked(values, q):
         v_hi, v_lo = split(values)
-        both = lax.dot_general(
-            jnp.concatenate([v_hi, v_lo], axis=0), pack_w[q], (((1,), (1,)), ((), ())),
-            preferred_element_type=f32)
+        both = dot(jnp.concatenate([v_hi, v_lo], axis=0), pack_w[q])
         return both[:40] + both[40:]
 
+    t_mix(2)
     fix = unpacked(sol[...], me_s)
     for k in range(1, parts):
         back_copy(k).wait_recv()
     for k in range(1, parts):
         fix = fix + unpacked(low_back[k], lax.rem(me_s + k, parts))
-    fix = lane_cat([fix[8 * i:8 * i + 8] for i in range(5)])
-    hi = fix.astype(bf16).astype(f32)
-    fix = jnp.concatenate([hi, hi, fix - hi], axis=0).astype(bf16)
-    c = c + dot(mat("p32"), fix)
-
-    c = c + tau * mid_residual(4, 5, mid_t[3], c)
-    t_start(6, mid_t[4], c)
+
+    low_start(6, fix)
+    c = c + from_low(fix)
+    table = s_start(4, c, "e3")
+    part = flux(c, jm, "d3")
+    t_mix(6)
+    jump = s_local(table)
+    part = rhs - t_finish(4, rows_m) - part - s_finish(4, jump, "et3")
+    c = c + tau * (part - from_low(t_finish(6, rows_l)[:40]))
+
+    t_start(7, c)
     corrected = smoothed + dot(mat("p43"), split_rows(c))
     table = s_start(5, corrected, "e4")
     part = flux(corrected, jac, "d4")
+    t_mix(7)
     jump = s_local(table)
-    t_mix(6, mid_t[4])
     part = g - part - s_finish(5, jump, "et4")
-    part = part - t_finish(2, fine_t[1], rows_f)
-    coupled = dot(mat("p43"), split_rows(t_finish(6, mid_t[4], rows_m)))
+    part = part - t_finish(2, rows_f)
+    coupled = dot(mat("p43"), split_rows(t_finish(7, rows_m)))
     result = corrected + tau * (part - coupled)
     for i in range(5):
         out[i] = result[:, columns * i:columns * (i + 1)]
 
-    order = [fine_t[0], mid_t[0], fine_t[1], mid_t[1], mid_t[2], mid_t[3], mid_t[4]]
-    for number, bufs in enumerate(order):
+    for number, bufs in enumerate(bufs_t):
         all_of(bufs[0], t_send.at[number])
         all_of(bufs[2], b_send.at[number])
     for number in range(6):
@@ -403,23 +440,39 @@
     wide = -(-cols // LANES) * LANES
     width = 5 * columns
     faces = 6 * columns
-    vmem = pl.BlockSpec(memory_space=pltpu.VMEM)
-
-    def time_buffers(rows):
-        return [pltpu.VMEM((nt, rows // nt, width), f32) for _ in range(4)]
-
-    scratch = [
+    operands = (
+        adjoint.reshape(5, 64, columns),
+        gradient.reshape(5, 64, columns),
+        jacobian.reshape(15, 5, 64, columns),
+        pseudo_step,
+        send_list.reshape(1, 2 * slots),
+        face_source,
+        coarse_owner.reshape(1, columns),
+        coarse_inv.reshape(40, 40, cols),
+        jnp.asarray(table),
+    )
+
+    low_piece = -(-40 // nt)
+
+    def time_buffers(piece, lanes):
+        return [pltpu.VMEM((nt, piece, lanes), f32) for _ in range(4)]
+
+    scratch = [pltpu.VMEM(x.shape, x.dtype) for x in operands]
+    scratch += [
+        pltpu.SemaphoreType.DMA((len(operands),)),
         pltpu.VMEM((15, 5, 32, columns), f32),
         pltpu.VMEM((faces, 2 * slots), bf16),
         pltpu.VMEM((faces, faces), bf16),
         pltpu.VMEM((2 * slots, faces), bf16),
-        pltpu.VMEM((parts, columns, wide), bf16),
+        pltpu.VMEM((parts, wide, columns), bf16),
         pltpu.VMEM((64, width), f32),
         pltpu.VMEM((32, width), f32),
+        pltpu.VMEM((low_piece * nt, columns), f32),
         pltpu.VMEM((40, wide), f32),
     ]
-    for rows in (64, 64, 32, 32, 32, 32, 32):
-        scratch += time_buffers(rows)
+    fine, mid, low = (64 // nt, width), (32 // nt, width), (low_piece, columns)
+    for piece, lanes in (fine, mid, fine, mid, mid, low, low, mid):
+        scratch += time_buffers(piece, lanes)
     scratch += [
         pltpu.VMEM((6, 2, 80, slots), f32),
         pltpu.VMEM((6, 2, 80, slots), f32),
@@ -428,27 +481,17 @@
         pltpu.VMEM((parts, 40, wide), f32),
     ]
     dma = pltpu.SemaphoreType.DMA
-    scratch += [dma((7,)) for _ in range(4)] + [dma((6, 2)) for _ in range(2)]
+    scratch += [dma((8,)) for _ in range(4)] + [dma((6, 2)) for _ in range(2)]
     scratch += [dma((parts,)) for _ in range(4)]
     result = pl.pallas_call(
         functools.partial(kernel, nt, parts, cols // parts, where, row),
         out_shape=jax.ShapeDtypeStruct((5, 64, columns), f32),
-        in_specs=[vmem] * 9,
-        out_specs=vmem,
+        in_specs=[pl.BlockSpec(memory_space=pltpu.HBM)] * len(operands),
+        out_specs=pl.BlockSpec(memory_space=pltpu.VMEM),
         scratch_shapes=scratch,
         compiler_params=pltpu.CompilerParams(
-            collective_id=0, has_side_effects=True, vmem_limit_bytes=50 * 1024 * 1024),
-    )(
-        adjoint.reshape(5, 64, columns),
-        gradient.reshape(5, 64, columns),
-        jacobian.reshape(15, 5, 64, columns),
-        pseudo_step,
-        send_list.reshape(1, 2 * slots),
-        face_source,
-        coarse_owner,
-        coarse_inv.reshape(40, 40, cols),
-        jnp.asarray(table),
-    )
+            collective_id=0, has_side_effects=True, vmem_limit_bytes=63 * 1024 * 1024),
+    )(*operands)
     return result.reshape(adjoint.shape)
 
 

time: 82.1 us -> 75.7 us (0.922)
  local copies, waits for them, and re-layouts: 7.81 us -> 1.59 us
    unnamed x16 -> x1, local copies, waits for them, and re-layouts: 7.81 us -> 1.59 us
where the time goes in v1:
time: 75.7 us; the launch traced here: 75.5 us
  Pallas kernels  73.9 us (98%)
  local copies, waits for them, and re-layouts  1.59 us (2%)
    pallas_call x1, Pallas kernels, on_device(): pl.pallas_call(functools.partial(kernel, nt, parts, cols // parts, where,...  73.9 us
    unnamed x1, local copies, waits for them, and re-layouts  1.59 us

profile of v1, /device:TPU:0, one launch (start us, length us, event | category | flops | bytes accessed | tf_op | source)
XLA Modules:
  0.0 75.5 jit_solution(6155844757482740361)
XLA Ops:
  0.0 73.9 %shard_map.91 = f32[5,64,128]{2,1,0:T(8,128)} custom-call(f32[5,64,128]{2,1,0:T(8,128)} %bitcast.10, f32[5,64,128]{2,1,0:T(8,128)} %bitcast.11, f32[15,5,64,128]{3,2,1,0:T(8,128)} %bitcast.7, f32[1,128]{1,0:T(1,128)} %refs_3_.1, s32[1,256]{1,0:T(1,128)} %bitcast.12, s32[6,128]{1,0:T(8,128)} %refs_5_.1, s32[1,128]{1,0:T(1,128)} %bitcast.13, ...), custom_call_target="tpu_custom_call" | custom-call | tf_op jit(solution)/shard_map/pallas_call | solution.py:486
  73.9 1.6 %copy.11 = f32[1,5,4,4,4,128]{5,4,3,2,1,0:T(4,128)} copy(f32[1,5,4,4,4,128]{5,4,3,2,1,0:T(4,128)} %bitcast.9) | data formatting | bytes 327680

commit v2 on v1

--- a/solution.py
+++ b/solution.py
@@ -144,6 +144,9 @@
     trace_out, trace_in, low_out, low_in, low_back = rest[32:37]
     t_send, t_recv, b_send, b_recv, h_send, h_recv, c_send, c_recv, g_send, g_recv = rest[37:]
     me_t, me_s = lax.axis_index("tm"), lax.axis_index("space")
+    holders, first = nt // 2, nt // 4
+    held_id = me_t - first
+    is_holder = jnp.logical_and(held_id >= 0, held_id < holders)
     columns = LANES
     width = 5 * columns
     slots = send_ref.shape[1] // 2
@@ -172,46 +175,66 @@
     def t_start(number, v):
         stage, landed, mixed, back = bufs_t[number]
         piece = stage.shape[1]
-        for k in range(nt):
-            stage[k] = v[piece * k:piece * (k + 1), :]
-        for k in far_first:
-            to = lax.rem(me_t + k, nt)
-            pltpu.make_async_remote_copy(
-                src_ref=stage.at[to], dst_ref=landed.at[nt - k], send_sem=t_send.at[number],
-                recv_sem=t_recv.at[number], device_id={"tm": to}, device_id_type=MESH).start()
-        landed[0] = stage[me_t]
-
-    def all_of(buf, sem):
-        view = buf.at[pl.ds(1, nt - 1)]
+        for h in range(holders):
+            stage[h] = v[piece * h:piece * (h + 1), :]
+        for k in range(holders):
+            h = lax.rem(me_t + k, holders)
+            to = first + h
+
+            @pl.when(to != me_t)
+            def _(h=h, to=to):
+                pltpu.make_async_remote_copy(
+                    src_ref=stage.at[h], dst_ref=landed.at[lax.rem(me_t - to + nt, nt)],
+                    send_sem=t_send.at[number], recv_sem=t_recv.at[number],
+                    device_id={"tm": to}, device_id_type=MESH).start()
+
+        @pl.when(is_holder)
+        def _():
+            landed[0] = stage[held_id]
+
+    def take(buf, count, sem):
+        view = buf.at[pl.ds(0, count)]
         pltpu.make_async_copy(view, view, sem).wait()
+
+    def take_holders(buf, sem):
+        @pl.when(is_holder)
+        def _():
+            take(buf, holders - 1, sem)
+
+        @pl.when(jnp.logical_not(is_holder))
+        def _():
+            take(buf, holders, sem)
 
     def t_mix(number):
         stage, landed, mixed, back = bufs_t[number]
-        all_of(landed, t_recv.at[number])
-
-        def block(b, carry):
-            lanes = pl.ds(pl.multiple_of(b * LANES, LANES), LANES)
-            y = landed[:, :, lanes]
-            total = row[0] * y
-            for m in range(1, nt):
-                total = total + row[m] * jnp.concatenate([y[m:], y[:m]], axis=0)
-            mixed[:, :, lanes] = total
-            return carry
-
-        lax.fori_loop(0, landed.shape[2] // LANES, block, 0)
-        for k in far_first:
-            to = lax.rem(me_t + k, nt)
-            pltpu.make_async_remote_copy(
-                src_ref=mixed.at[k], dst_ref=back.at[me_t], send_sem=b_send.at[number],
-                recv_sem=b_recv.at[number], device_id={"tm": to}, device_id_type=MESH).start()
-        back[me_t] = mixed[0]
+
+        @pl.when(is_holder)
+        def _():
+            take(landed, nt - 1, t_recv.at[number])
+
+            def block(b, carry):
+                lanes = pl.ds(pl.multiple_of(b * LANES, LANES), LANES)
+                y = landed[:, :, lanes]
+                total = row[0] * y
+                for m in range(1, nt):
+                    total = total + row[m] * jnp.concatenate([y[m:], y[:m]], axis=0)
+                mixed[:, :, lanes] = total
+                return carry
+
+            lax.fori_loop(0, landed.shape[2] // LANES, block, 0)
+            for k in far_first:
+                to = lax.rem(me_t + k, nt)
+                pltpu.make_async_remote_copy(
+                    src_ref=mixed.at[k], dst_ref=back.at[held_id], send_sem=b_send.at[number],
+                    recv_sem=b_recv.at[number], device_id={"tm": to}, device_id_type=MESH).start()
+            back[held_id] = mixed[0]
 
     def t_finish(number, rows_ref):
         stage, landed, mixed, back = bufs_t[number]
-        all_of(back, b_recv.at[number])
+        take_holders(back, b_recv.at[number])
         piece = stage.shape[1]
-        for k in range(nt):
-            rows_ref[piece * k:piece * (k + 1), :] = back[k]
+        for h in range(holders):
+            rows_ref[piece * h:piece * (h + 1), :] = back[h]
         return rows_ref[...]
 
     def trace_copy(number, side):
@@ -422,8 +445,12 @@
         out[i] = result[:, columns * i:columns * (i + 1)]
 
     for number, bufs in enumerate(bufs_t):
-        all_of(bufs[0], t_send.at[number])
-        all_of(bufs[2], b_send.at[number])
+        take_holders(bufs[0], t_send.at[number])
+
+        @pl.when(is_holder)
+        def _(number=number, bufs=bufs):
+            take(bufs[2], nt - 1, b_send.at[number])
+
     for number in range(6):
         for side in range(2):
             trace_copy(number, side).wait_send()
@@ -452,10 +479,11 @@
         jnp.asarray(table),
     )
 
-    low_piece = -(-40 // nt)
+    holders = nt // 2
+    low_piece = -(-40 // holders)
 
     def time_buffers(piece, lanes):
-        return [pltpu.VMEM((nt, piece, lanes), f32) for _ in range(4)]
+        return [pltpu.VMEM((count, piece, lanes), f32) for count in (holders, nt, nt, holders)]
 
     scratch = [pltpu.VMEM(x.shape, x.dtype) for x in operands]
     scratch += [
@@ -467,10 +495,10 @@
         pltpu.VMEM((parts, wide, columns), bf16),
         pltpu.VMEM((64, width), f32),
         pltpu.VMEM((32, width), f32),
-        pltpu.VMEM((low_piece * nt, columns), f32),
+        pltpu.VMEM((low_piece * holders, columns), f32),
         pltpu.VMEM((40, wide), f32),
     ]
-    fine, mid, low = (64 // nt, width), (32 // nt, width), (low_piece, columns)
+    fine, mid, low = (64 // holders, width), (32 // holders, width), (low_piece, columns)
     for piece, lanes in (fine, mid, fine, mid, mid, low, low, mid):
         scratch += time_buffers(piece, lanes)
     scratch += [

time: 75.7 us -> 71.5 us (0.945)
  Pallas kernels: 73.9 us -> 69.7 us
    pallas_call x1, Pallas kernels: 73.9 us -> 69.7 us  [on_device(): pl.pallas_call(functools.partial(kernel, nt, parts, cols // parts, where,...]
where the time goes in v2:
time: 71.5 us; the launch traced here: 71.3 us
  Pallas kernels  69.7 us (97%)
  local copies, waits for them, and re-layouts  1.59 us (2%)
    pallas_call x1, Pallas kernels, on_device(): pl.pallas_call(functools.partial(kernel, nt, parts, cols // parts, where,...  69.7 us
    unnamed x1, local copies, waits for them, and re-layouts  1.59 us

profile of v2, /device:TPU:0, one launch (start us, length us, event | category | flops | bytes accessed | tf_op | source)
XLA Modules:
  0.0 71.3 jit_solution(13307833719600998944)
XLA Ops:
  0.0 69.7 %shard_map.91 = f32[5,64,128]{2,1,0:T(8,128)} custom-call(f32[5,64,128]{2,1,0:T(8,128)} %bitcast.10, f32[5,64,128]{2,1,0:T(8,128)} %bitcast.11, f32[15,5,64,128]{3,2,1,0:T(8,128)} %bitcast.7, f32[1,128]{1,0:T(1,128)} %refs_3_.1, s32[1,256]{1,0:T(1,128)} %bitcast.12, s32[6,128]{1,0:T(8,128)} %refs_5_.1, s32[1,128]{1,0:T(1,128)} %bitcast.13, ...), custom_call_target="tpu_custom_call" | custom-call | tf_op jit(solution)/shard_map/pallas_call | solution.py:514
  69.7 1.6 %copy.11 = f32[1,5,4,4,4,128]{5,4,3,2,1,0:T(4,128)} copy(f32[1,5,4,4,4,128]{5,4,3,2,1,0:T(4,128)} %bitcast.9) | data formatting | bytes 327680

commit v3 on v2

--- a/solution.py
+++ b/solution.py
@@ -366,7 +366,6 @@
 
     low_start(5, to_low(c))
     table = s_start(3, c, "e3")
-    t_start(4, c)
     part = flux(c, jm, "d3")
     t_mix(5)
     jump = s_local(table)
@@ -394,8 +393,8 @@
     for k in range(1, parts):
         low_out[k] = packed_for(lax.rem(me_s + k, parts))
         low_copy(k).start()
+    t_start(4, c)
     t_start(2, smoothed)
-    t_mix(4)
     arrived = packed_for(me_s)
     for k in range(1, parts):
         low_copy(k).wait_recv()
@@ -415,7 +414,7 @@
         both = dot(jnp.concatenate([v_hi, v_lo], axis=0), pack_w[q])
         return both[:40] + both[40:]
 
-    t_mix(2)
+    t_mix(4)
     fix = unpacked(sol[...], me_s)
     for k in range(1, parts):
         back_copy(k).wait_recv()
@@ -427,6 +426,7 @@
     table = s_start(4, c, "e3")
     part = flux(c, jm, "d3")
     t_mix(6)
+    t_mix(2)
     jump = s_local(table)
     part = rhs - t_finish(4, rows_m) - part - s_finish(4, jump, "et3")
     c = c + tau * (part - from_low(t_finish(6, rows_l)[:40]))

time: 71.5 us -> 69.1 us (0.966)
  Pallas kernels: 69.7 us -> 67.4 us
    pallas_call x1, Pallas kernels: 69.7 us -> 67.4 us  [on_device(): pl.pallas_call(functools.partial(kernel, nt, parts, cols // parts, where,...]
where the time goes in v3:
time: 69.1 us; the launch traced here: 69 us
  Pallas kernels  67.4 us (98%)
  local copies, waits for them, and re-layouts  1.59 us (2%)
    pallas_call x1, Pallas kernels, on_device(): pl.pallas_call(functools.partial(kernel, nt, parts, cols // parts, where,...  67.4 us
    unnamed x1, local copies, waits for them, and re-layouts  1.59 us

profile of v3, /device:TPU:0, one launch (start us, length us, event | category | flops | bytes accessed | tf_op | source)
XLA Modules:
  0.0 69.0 jit_solution(3357232647807981969)
XLA Ops:
  0.0 67.4 %shard_map.91 = f32[5,64,128]{2,1,0:T(8,128)} custom-call(f32[5,64,128]{2,1,0:T(8,128)} %bitcast.10, f32[5,64,128]{2,1,0:T(8,128)} %bitcast.11, f32[15,5,64,128]{3,2,1,0:T(8,128)} %bitcast.7, f32[1,128]{1,0:T(1,128)} %refs_3_.1, s32[1,256]{1,0:T(1,128)} %bitcast.12, s32[6,128]{1,0:T(8,128)} %refs_5_.1, s32[1,128]{1,0:T(1,128)} %bitcast.13, ...), custom_call_target="tpu_custom_call" | custom-call | tf_op jit(solution)/shard_map/pallas_call | solution.py:514
  67.4 1.6 %copy.11 = f32[1,5,4,4,4,128]{5,4,3,2,1,0:T(4,128)} copy(f32[1,5,4,4,4,128]{5,4,3,2,1,0:T(4,128)} %bitcast.9) | data formatting | bytes 327680
